TPU v7x, 32 devices: a whole 2x2x4 slice. The times are simulated.
32 devices in a mesh: tm: 8 (over z, y), ep: 4 (over x, core).
Axes of the slice: x: 2, y: 2, z: 4, core: 2. Of those that a mesh axis runs over, the one named last changes fastest.
Arguments:
- queries: bfloat16 [4096, 1024], P(('tm', 'ep')), may hold values from -256 to 256
- keys: bfloat16 [4096, 1024], P(('tm', 'ep')), may hold values from -6 to 6
- values: bfloat16 [4096, 1024], P(('tm', 'ep')), may hold values from -6 to 6
- stream: bfloat16 [4096, 1024], P(('tm', 'ep')), may hold values from -16 to 16
- grad_out: bfloat16 [4096, 1024], P(('tm', 'ep')), may hold values from -6 to 6
- norm_gain: float32 [1024], replicated, may hold values from 0.1 to 1.9
- gate_probs: float32 [4096, 2], P(('tm', 'ep')), may hold values from 0.1 to 0.9
- routes: int32 [4096, 2], P(('tm', 'ep')), may hold values from 0 to 7, all different within a row; in each aligned block of 128 rows (0 to 127, 128 to 255, ...) at most 48 rows name the same one
- w_gate: bfloat16 [8, 1024, 4096], P('tm', None, 'ep'), may hold values from -0.1875 to 0.1875
- w_up: bfloat16 [8, 1024, 4096], P('tm', None, 'ep'), may hold values from -0.1875 to 0.1875
- w_down: bfloat16 [8, 4096, 1024], P('tm', 'ep'), may hold values from -0.09375 to 0.09375
Outputs:
- queries_grad: bfloat16 [4096, 1024], P(('tm', 'ep'))
- keys_grad: bfloat16 [4096, 1024], P(('tm', 'ep'))
- values_grad: bfloat16 [4096, 1024], P(('tm', 'ep'))
- stream_grad: bfloat16 [4096, 1024], P(('tm', 'ep'))
- gate_weight_grad: float32 [8, 1024, 4096], P('tm', None, 'ep')
- up_weight_grad: float32 [8, 1024, 4096], P('tm', None, 'ep')
- down_weight_grad: float32 [8, 4096, 1024], P('tm', 'ep')
Inputs may be any that keep to these rules, and one draw needn't show every extreme that they name: `routes`: in the frames of one device no expert is named by more than 48 frames, a bound that some block reaches.
All inputs are finite; a program needn't handle non-finite values.
Results may differ from a plain program's by a relative error of at most 0.015.
Values may be sent and summed in bfloat16 or wider, within the bound.
A program may use at most 128 MiB of HBM per device.

v0:
```python
import functools
import math

import jax
import jax.numpy as jnp
from jax import lax
from jax.experimental import pallas as pl
from jax.experimental.pallas import tpu as pltpu
from jax.sharding import PartitionSpec as P

D = 1024
HEADS = 16
HEAD = 64
SPAN = 64
LEFT = 256


EPSILON = 1e-06


def shifted(block, axis, distance):
    devices = range(lax.axis_size(axis))
    route = [(i - distance, i) for i in devices if i - distance in devices]
    return lax.ppermute(block, axis, route)


MESH = pl.DeviceIdType.MESH
CHUNKS = 4
TILE = 256


def nt(a, b):
    return lax.dot_general(a, b, (((1,), (1,)), ((), ())), preferred_element_type=jnp.float32)


def tn(a, b):
    return lax.dot_general(a, b, (((0,), (0,)), ((), ())), preferred_element_type=jnp.float32)


def expert_kernel(
    n, cap,
    pick_ref, pick_t_ref, prob_ref, stream_ref, grad_ref, gain_ref, wg_hbm, wu_hbm, wd_hbm,
    sgrad_ref, gg_hbm, ug_hbm, dg_hbm,
    norm_s, send, xg, wg, wu, wd, acted, dgate, dup, part, from_core, from_x, back, grads,
    w_sem, out_sem, loc_sem, d_send, d_recv, a_send, a_recv, b_send, b_recv, c_send, c_recv,
):
    i = lax.axis_index("tm")
    j = lax.axis_index("ep")
    j1 = j + 1 - 2 * (j % 2)
    j2 = (j + 2) % 4
    j3 = (j1 + 2) % 4
    width = stream_ref.shape[1]
    hidden = wg.shape[1]
    per = n // CHUNKS
    rows = per * 4 * cap

    weights = [
        pltpu.make_async_copy(src, dst, w_sem.at[q])
        for q, (src, dst) in enumerate(((wg_hbm, wg), (wu_hbm, wu), (wd_hbm, wd)))
    ]
    for copy in weights:
        copy.start()

    barrier = pltpu.get_barrier_semaphore()
    for d in range(1, n):
        pl.semaphore_signal(barrier, inc=1, device_id=((i + d) % n, j), device_id_type=MESH)
    pl.semaphore_signal(barrier, inc=1, device_id=(i, j1), device_id_type=MESH)
    pl.semaphore_signal(barrier, inc=1, device_id=(i, j2), device_id_type=MESH)

    stream_f = stream_ref[...].astype(jnp.float32)
    inverse_rms = lax.rsqrt(jnp.mean(stream_f * stream_f, -1, keepdims=True) + EPSILON)
    norm_s[...] = (stream_f * inverse_rms * gain_ref[...]).astype(jnp.bfloat16)

    pl.semaphore_wait(barrier, n + 1)

    def remote(src, dst, ssem, rsem, to):
        return pltpu.make_async_remote_copy(
            src_ref=src, dst_ref=dst, send_sem=ssem, recv_sem=rsem, device_id=to, device_id_type=MESH
        )

    def to_expert(d):
        return remote(send.at[d], xg.at[d, j], d_send.at[d, 0], d_recv.at[d, 0], ((i + d) % n, j))

    own_copy = pltpu.make_async_copy(send.at[0], xg.at[0, j], loc_sem)
    for d in list(range(1, n)) + [0]:
        e = (i + d) % n
        pick = pick_ref[e]
        send[d, 0] = jnp.dot(pick, norm_s[...], preferred_element_type=jnp.float32).astype(jnp.bfloat16)
        grad_rows = jnp.dot(pick, grad_ref[...], preferred_element_type=jnp.float32)
        send[d, 1] = (grad_rows * prob_ref[e]).astype(jnp.bfloat16)
        if d:
            to_expert(d).start()
        else:
            own_copy.start()

    def own_to_core(d):
        return remote(xg.at[d, j], xg.at[d, j], d_send.at[d, 1], d_recv.at[d, 1], (i, j1))

    def own_to_x(d):
        return remote(xg.at[d, j], xg.at[d, j], d_send.at[d, 2], d_recv.at[d, 2], (i, j2))

    def x_to_core(d):
        return remote(xg.at[d, j2], xg.at[d, j2], d_send.at[d, 3], d_recv.at[d, 3], (i, j1))

    def span(c):
        return range(c * per, (c + 1) * per)

    def forward_own(c):
        for d in span(c):
            if d:
                to_expert(d).wait_recv()
            else:
                own_copy.wait()
            own_to_x(d).start()
            own_to_core(d).start()

    def forward_x(c):
        for d in span(c):
            own_to_x(d).wait_recv()
            x_to_core(d).start()

    def gather(c):
        for d in span(c):
            own_to_core(d).wait_recv()
            x_to_core(d).wait_recv()

    def compute(c):
        here = pl.ds(c * rows, rows)

        @pl.loop(0, hidden // TILE)
        def _(t):
            cols = pl.ds(pl.multiple_of(t * TILE, TILE), TILE)
            x = xg[c * per : (c + 1) * per, :, 0].reshape(rows, width)
            g = xg[c * per : (c + 1) * per, :, 1].reshape(rows, width)
            gate_pre = jnp.dot(x, wg[:, cols], preferred_element_type=jnp.float32)
            up_pre = jnp.dot(x, wu[:, cols], preferred_element_type=jnp.float32)
            dact = nt(g, wd[cols, :])
            sig = jax.nn.sigmoid(gate_pre)
            silu = gate_pre * sig
            acted[here, cols] = (silu * up_pre).astype(jnp.bfloat16)
            dgate[here, cols] = (dact * up_pre * sig * (1.0 + gate_pre * (1.0 - sig))).astype(jnp.bfloat16)
            dup[here, cols] = (dact * silu).astype(jnp.bfloat16)

        @pl.loop(0, width // TILE)
        def _(t):
            cols = pl.ds(pl.multiple_of(t * TILE, TILE), TILE)
            dx = nt(dgate[here, :], wg[cols, :]) + nt(dup[here, :], wu[cols, :])
            part[c * per : (c + 1) * per, :, :, cols] = dx.astype(jnp.bfloat16).reshape(per, 4, cap, TILE)

    def core_copies(d):
        return (
            remote(part.at[d, j1], from_core.at[d, 0], a_send.at[d, 0], a_recv.at[d, 0], (i, j1)),
            remote(part.at[d, j3], from_core.at[d, 1], a_send.at[d, 1], a_recv.at[d, 1], (i, j1)),
        )

    def x_copy(d):
        return remote(part.at[d, j2], from_x.at[d], b_send.at[d], b_recv.at[d], (i, j2))

    def home_copy(d):
        return remote(part.at[d, j], back.at[i], c_send.at[d], c_recv.at[d], ((i + n - d) % n, j))

    def stage_a(c):
        for d in span(c):
            for copy in core_copies(d):
                copy.start()

    def stage_b(c):
        for d in span(c):
            core_copies(d)[1].wait_recv()
            total = part[d, j2].astype(jnp.float32) + from_core[d, 1].astype(jnp.float32)
            part[d, j2] = total.astype(jnp.bfloat16)
            x_copy(d).start()

    def stage_c(c):
        for d in span(c):
            core_copies(d)[0].wait_recv()
            x_copy(d).wait_recv()
            total = part[d, j].astype(jnp.float32) + from_core[d, 0].astype(jnp.float32)
            total = (total + from_x[d].astype(jnp.float32)).astype(jnp.bfloat16)
            if d:
                part[d, j] = total
                home_copy(d).start()
            else:
                back[i] = total

    forward_own(0)
    for copy in weights:
        copy.wait()
    forward_own(1)
    for c in range(CHUNKS):
        forward_x(c)
        gather(c)
        compute(c)
        stage_a(c)
        if c + 2 < CHUNKS:
            forward_own(c + 2)
        if c >= 1:
            stage_b(c - 1)
        if c >= 2:
            stage_c(c - 2)
    stage_b(CHUNKS - 1)

    total_rows = n * 4 * cap
    writes = [
        pltpu.make_async_copy(grads.at[q], dst, out_sem.at[q]) for q, dst in enumerate((dg_hbm, gg_hbm, ug_hbm))
    ]

    @pl.loop(0, hidden // TILE)
    def _(t):
        cols = pl.ds(pl.multiple_of(t * TILE, TILE), TILE)
        lhs = acted[:, cols]
        for q in range(0, width, 512):
            rhs = xg[:, :, 1, :, q : q + 512].reshape(total_rows, 512)
            grads[0, cols, q : q + 512] = tn(lhs, rhs)

    writes[0].start()
    stage_c(CHUNKS - 2)
    stage_c(CHUNKS - 1)

    @pl.loop(0, width // TILE)
    def _(t):
        cols = pl.ds(pl.multiple_of(t * TILE, TILE), TILE)
        lhs = xg[:, :, 0, :, cols].reshape(total_rows, TILE)
        for q in range(0, hidden, 512):
            grads[1, cols, q : q + 512] = tn(lhs, dgate[:, q : q + 512])
            grads[2, cols, q : q + 512] = tn(lhs, dup[:, q : q + 512])

    writes[1].start()
    writes[2].start()

    for d in range(1, n):
        home_copy(d).wait_recv()
    dnormed = jnp.dot(pick_t_ref[...], back[...].reshape(n * cap, width), preferred_element_type=jnp.float32)
    stream_f = stream_ref[...].astype(jnp.float32)
    inverse_rms = lax.rsqrt(jnp.mean(stream_f * stream_f, -1, keepdims=True) + EPSILON)
    scaled = stream_f * inverse_rms
    weighted = dnormed * gain_ref[...]
    dstream = inverse_rms * (weighted - scaled * jnp.mean(weighted * scaled, -1, keepdims=True))
    sgrad_ref[...] = (grad_ref[...].astype(jnp.float32) + dstream).astype(jnp.bfloat16)

    for d in range(n):
        if d:
            to_expert(d).wait_send()
            home_copy(d).wait_send()
        own_to_core(d).wait_send()
        own_to_x(d).wait_send()
        x_to_core(d).wait_send()
        for copy in core_copies(d):
            copy.wait_send()
        x_copy(d).wait_send()
    for copy in writes:
        copy.wait()


def expert_part(n, cap, pick, pick_t, prob, stream, grad_out, gain, w_gate, w_up, w_down):
    frames, width = stream.shape
    hidden = w_gate.shape[1]
    total = n * 4 * cap
    bf, f32 = jnp.bfloat16, jnp.float32
    vmem = pl.BlockSpec(memory_space=pltpu.VMEM)
    hbm = pl.BlockSpec(memory_space=pl.ANY)
    dma = pltpu.SemaphoreType.DMA
    return pl.pallas_call(
        functools.partial(expert_kernel, n, cap),
        out_shape=(
            jax.ShapeDtypeStruct((frames, width), bf),
            jax.ShapeDtypeStruct((width, hidden), f32),
            jax.ShapeDtypeStruct((width, hidden), f32),
            jax.ShapeDtypeStruct((hidden, width), f32),
        ),
        in_specs=[vmem] * 6 + [hbm] * 3,
        out_specs=(vmem, hbm, hbm, hbm),
        scratch_shapes=[
            pltpu.VMEM((frames, width), bf),
            pltpu.VMEM((n, 2, cap, width), bf),
            pltpu.VMEM((n, 4, 2, cap, width), bf),
            pltpu.VMEM((width, hidden), bf),
            pltpu.VMEM((width, hidden), bf),
            pltpu.VMEM((hidden, width), bf),
            pltpu.VMEM((total, hidden), bf),
            pltpu.VMEM((total, hidden), bf),
            pltpu.VMEM((total, hidden), bf),
            pltpu.VMEM((n, 4, cap, width), bf),
            pltpu.VMEM((n, 2, cap, width), bf),
            pltpu.VMEM((n, cap, width), bf),
            pltpu.VMEM((n, cap, width), bf),
            pltpu.VMEM((3, width, hidden), f32),
            dma((3,)),
            dma((3,)),
            dma,
            dma((n, 4)),
            dma((n, 4)),
            dma((n, 2)),
            dma((n, 2)),
            dma((n,)),
            dma((n,)),
            dma((n,)),
            dma((n,)),
        ],
        compiler_params=pltpu.CompilerParams(
            collective_id=0, has_side_effects=True, vmem_limit_bytes=60 * 1024 * 1024
        ),
        cost_estimate=pl.CostEstimate(
            flops=16 * total * width * hidden, bytes_accessed=20 * width * hidden, transcendentals=0
        ),
    )(pick, pick_t, prob, stream, grad_out, gain, w_gate, w_up, w_down)


def attend_grads(query_rows, key_rows, value_rows, grad_rows, allowed):
    n_query = query_rows.shape[0]
    n_key = key_rows.shape[0]
    score_scale = 1.0 / math.sqrt(HEAD)
    q_three = query_rows.reshape(n_query, HEADS, HEAD)
    k_three = key_rows.reshape(n_key, HEADS, HEAD)
    v_three = value_rows.reshape(n_key, HEADS, HEAD)
    o_three = grad_rows.reshape(n_query, HEADS, HEAD)
    scores = (
        jnp.einsum("qhd,khd->hqk", q_three, k_three, preferred_element_type=jnp.float32)
        * score_scale
    )
    scores = jnp.where(allowed[None], scores, -jnp.inf)
    row_max = jnp.max(scores, -1, keepdims=True)
    exp_scores = jnp.exp(scores - row_max)
    probabilities = exp_scores / jnp.sum(exp_scores, -1, keepdims=True)
    pround = probabilities.astype(jnp.bfloat16)
    attn = jnp.einsum("hqk,khd->qhd", pround, v_three, preferred_element_type=jnp.float32)
    row_delta = jnp.sum(o_three.astype(jnp.float32) * attn, -1)
    dprob = jnp.einsum("qhd,khd->hqk", o_three, v_three, preferred_element_type=jnp.float32)
    dscore = (probabilities * (dprob - row_delta.T[:, :, None])).astype(jnp.bfloat16)
    grad_q = (
        jnp.einsum("hqk,khd->qhd", dscore, k_three, preferred_element_type=jnp.float32)
        * score_scale
    )
    grad_k = (
        jnp.einsum("hqk,qhd->khd", dscore, q_three, preferred_element_type=jnp.float32)
        * score_scale
    )
    grad_v = jnp.einsum("hqk,qhd->khd", pround, o_three, preferred_element_type=jnp.float32)
    return (grad_q.reshape(n_query, D), grad_k.reshape(n_key, D), grad_v.reshape(n_key, D))


def body(
    queries, keys, values, stream, grad_out, norm_gain, gate_probs, routes, w_gate, w_up, w_down
):
    frames = queries.shape[0]
    model_width = queries.shape[1]
    top_count = routes.shape[1]
    experts = lax.axis_size("tm")
    ep_count = lax.axis_size("ep")
    capacity = 3 * frames * top_count // (2 * experts)
    cap = -(-capacity // 16) * 16
    names = jnp.arange(experts, dtype=jnp.int32)[None, :]
    chosen = [(routes[:, k : k + 1] == names).astype(jnp.float32) for k in range(top_count)]
    order = jnp.arange(frames, dtype=jnp.int32)
    earlier = (order[None, :] < order[:, None]).astype(jnp.bfloat16)
    before = jnp.dot(earlier, sum(chosen).astype(jnp.bfloat16), preferred_element_type=jnp.float32)
    row_ids = jnp.arange(experts * cap, dtype=jnp.int32)[:, None]
    hits = []
    for k in range(top_count):
        slot = jnp.sum(before * chosen[k], 1).astype(jnp.int32)
        hits.append((routes[:, k] * cap + slot)[None, :] == row_ids)
    pick = functools.reduce(jnp.logical_or, hits).astype(jnp.bfloat16)
    prob = sum(
        jnp.sum(jnp.where(hits[k], gate_probs[:, k][None, :], 0.0), 1, keepdims=True)
        for k in range(top_count)
    )
    stream_grad, gate_grad, up_grad, down_grad = expert_part(
        experts,
        cap,
        pick.reshape(experts, cap, frames),
        pick.T,
        prob.reshape(experts, cap, 1),
        stream,
        grad_out,
        norm_gain[None, :],
        w_gate[0],
        w_up[0],
        w_down[0],
    )
    reach = -(-LEFT // frames)
    arrived = [
        shifted((keys, values), ("tm", "ep"), reach - offset_index) for offset_index in range(reach)
    ]
    rim_keys = jnp.concatenate([piece[0] for piece in arrived], 0)
    rim_values = jnp.concatenate([piece[1] for piece in arrived], 0)
    key_rows = jnp.concatenate([rim_keys, keys], 0)
    value_rows = jnp.concatenate([rim_values, values], 0)
    position = lax.axis_index("tm") * ep_count + lax.axis_index("ep")
    base_frame = position * frames
    query_pos = base_frame + jnp.arange(frames, dtype=jnp.int32)
    key_pos = base_frame - LEFT + jnp.arange(LEFT + frames, dtype=jnp.int32)
    query_span = query_pos // SPAN
    allowed = jnp.logical_and(
        key_pos[None, :] >= 0, key_pos[None, :] >= (query_span * SPAN - LEFT)[:, None]
    )
    allowed = jnp.logical_and(allowed, key_pos[None, :] < ((query_span + 1) * SPAN)[:, None])
    grad_q, grad_k, grad_v = attend_grads(queries, key_rows, value_rows, stream_grad, allowed)
    spare = reach * frames - LEFT
    padded_k = jnp.concatenate([jnp.zeros((spare, model_width), jnp.float32), grad_k[:LEFT]], 0)
    padded_v = jnp.concatenate([jnp.zeros((spare, model_width), jnp.float32), grad_v[:LEFT]], 0)
    sent_back = [
        (
            shifted(
                padded_k[offset_index * frames : (offset_index + 1) * frames].astype(jnp.bfloat16),
                ("tm", "ep"),
                offset_index - reach,
            ).astype(jnp.float32),
            shifted(
                padded_v[offset_index * frames : (offset_index + 1) * frames].astype(jnp.bfloat16),
                ("tm", "ep"),
                offset_index - reach,
            ).astype(jnp.float32),
        )
        for offset_index in range(reach)
    ]
    keys_total = grad_k[LEFT:]
    values_total = grad_v[LEFT:]
    for piece in sent_back:
        keys_total = keys_total + piece[0]
        values_total = values_total + piece[1]
    return (
        grad_q.astype(jnp.bfloat16),
        keys_total.astype(jnp.bfloat16),
        values_total.astype(jnp.bfloat16),
        stream_grad,
        gate_grad[None],
        up_grad[None],
        down_grad[None],
    )


def solution(mesh):
    return jax.shard_map(
        body,
        mesh=mesh,
        in_specs=(
            P(("tm", "ep"), None),
            P(("tm", "ep"), None),
            P(("tm", "ep"), None),
            P(("tm", "ep"), None),
            P(("tm", "ep"), None),
            P(),
            P(("tm", "ep"), None),
            P(("tm", "ep"), None),
            P("tm", None, "ep"),
            P("tm", None, "ep"),
            P("tm", "ep", None),
        ),
        out_specs=(
            P(("tm", "ep"), None),
            P(("tm", "ep"), None),
            P(("tm", "ep"), None),
            P(("tm", "ep"), None),
            P("tm", None, "ep"),
            P("tm", None, "ep"),
            P("tm", "ep", None),
        ),
        check_vma=False,
    )
```

profile of v0, /device:TPU:24, one launch (start us, length us, event | category | flops | bytes accessed | tf_op | source)
XLA Modules:
  0.0 166.6 jit_solution(12713825317030202276)
XLA Ops:
  0.6 1.9 %collective-permute-start.1 = (bf16[128,1024]{1,0:T(8,128)(2,1)}, bf16[128,1024]{1,0:T(8,128)(2,1)S(1)}, u32[]{:S(2)}, u32[]{:S(2)}) collective-permute-start(bf16[128,1024]{1,0:T(8,128)(2,1)} %param.12), channel_id=1, source_target_pairs={{0,1},{1,2},{2,3},{3,4},{4,5},{5,6},{6,7},{7,8},{8,9},{9,10},{10,1... | collective-permute-start | bytes 786440 | tf_op jit(solution)/shard_map/ppermute | solution.py:24
  2.6 3.4 %collective-permute-start = (bf16[128,1024]{1,0:T(8,128)(2,1)}, bf16[128,1024]{1,0:T(8,128)(2,1)S(1)}, u32[]{:S(2)}, u32[]{:S(2)}) collective-permute-start(bf16[128,1024]{1,0:T(8,128)(2,1)} %param.12), channel_id=1, source_target_pairs={{0,2},{1,3},{2,4},{3,5},{4,6},{5,7},{6,8},{7,9},{8,10},{9,11},{10,... | collective-permute-start | bytes 786440 | tf_op jit(solution)/shard_map/ppermute | solution.py:24
  6.0 3.2 %collective-permute-start.3 = (bf16[128,1024]{1,0:T(8,128)(2,1)}, bf16[128,1024]{1,0:T(8,128)(2,1)S(1)}, u32[]{:S(2)}, u32[]{:S(2)}) collective-permute-start(bf16[128,1024]{1,0:T(8,128)(2,1)} %param.13), channel_id=1, source_target_pairs={{0,1},{1,2},{2,3},{3,4},{4,5},{5,6},{6,7},{7,8},{8,9},{9,10},{10,1... | collective-permute-start | bytes 786440 | tf_op jit(solution)/shard_map/ppermute | solution.py:24
  9.2 3.4 %collective-permute-start.2 = (bf16[128,1024]{1,0:T(8,128)(2,1)}, bf16[128,1024]{1,0:T(8,128)(2,1)S(1)}, u32[]{:S(2)}, u32[]{:S(2)}) collective-permute-start(bf16[128,1024]{1,0:T(8,128)(2,1)} %param.13), channel_id=1, source_target_pairs={{0,2},{1,3},{2,4},{3,5},{4,6},{5,7},{6,8},{7,9},{8,10},{9,11},{10,... | collective-permute-start | bytes 786440 | tf_op jit(solution)/shard_map/ppermute | solution.py:24
  16.8 0.9 add.115.prob_ref
  17.7 96.6 %shard_map.162 = (bf16[128,1024]{1,0:T(8,128)(2,1)}, f32[1024,1024]{1,0:T(8,128)}, f32[1024,1024]{1,0:T(8,128)}, f32[1024,1024]{1,0:T(8,128)}) custom-call(bf16[8,48,128]{2,1,0:T(8,128)(2,1)} %or_convert_fusion.pick_ref, bf16[128,384]{1,0:T(8,128)(2,1)} %fusion.12.pick_t_ref, f32[8,48,1]{2,1,0:T(8,128)} %add.115.prob_ref, bf16[128,1024]{1,0:T(8,128)(2,1)} %stream_ref.1, ...), custom_call_target="tpu_custom_call" | custom-call | flops 25769803776 | bytes 20971520 | tf_op jit(solution)/shard_map/pallas_call | solution.py:263
  114.4 1.1 copy.57
  116.6 1.2 copy.54
  117.9 1.2 copy.58
  119.1 2.4 %fusion.20 = (f32[16,128]{1,0:T(8,128)S(1)}, f32[16,128,384]{1,2,0:T(8,128)S(1)}) fusion(pred[128,384]{0,1:T(8,128)(4,1)S(1)} %compare_and_fusion, bf16[384,16,64]{0,2,1:T(8,128)(2,1)} %bitcast.71, bf16[128,16,64]{0,2,1:T(8,128)(2,1)} %bitcast.80), kind=kOutput, calls=%fused_computation.60 | convolution fusion | flops 103809408 | bytes 4251648 | tf_op jit(solution)/shard_map/sub | solution.py:323
  121.9 1.3 copy-done.2
  123.2 2.0 %fusion.22 = (bf16[384,16,64]{0,2,1:T(8,128)(2,1)S(1)}, f32[384,16,64]{0,2,1:T(8,128)}) fusion(bf16[128,16,64]{0,2,1:T(8,128)(2,1)S(1)} %bitcast.75, bf16[16,128,384]{1,2,0:T(8,128)(2,1)S(1)} %fusion.5), kind=kOutput, calls=%fused_computation.62 | convolution fusion | flops 101056512 | bytes 4194304 | tf_op jit(solution)/shard_map/hqk,qhd->khd/dot_general | solution.py:338
  126.8 2.0 %fusion.21 = (bf16[384,16,64]{0,2,1:T(8,128)(2,1)S(1)}, f32[384,16,64]{0,2,1:T(8,128)}) fusion(bf16[16,128,384]{1,2,0:T(8,128)(2,1)S(1)} %multiply_convert_fusion, bf16[128,16,64]{0,2,1:T(8,128)(2,1)S(1)} %bitcast.81), kind=kOutput, calls=%fused_computation.61 | convolution fusion | flops 101449728 | bytes 4194304 | tf_op jit(solution)/shard_map/hqk,qhd->khd/dot_general | solution.py:335
  128.8 0.8 fusion.19
  129.6 1.9 %copy.65 = bf16[128,1024]{1,0:T(8,128)(2,1)} copy(bf16[128,1024]{0,1:T(8,128)(2,1)} %bitcast.85) | data formatting | bytes 524288 | tf_op jit(solution)/shard_map/convert_element_type | solution.py:404
  131.5 1.9 %collective-permute-start.5 = (bf16[128,1024]{1,0:T(8,128)(2,1)}, bf16[128,1024]{1,0:T(8,128)(2,1)}, u32[]{:S(2)}, u32[]{:S(2)}) collective-permute-start(bf16[128,1024]{1,0:T(8,128)(2,1)} %copy.65), channel_id=1, source_target_pairs={{1,0},{2,1},{3,2},{4,3},{5,4},{6,5},{7,6},{8,7},{9,8},{10,9},{11,1... | collective-permute-start | bytes 786440 | tf_op jit(solution)/shard_map/ppermute | solution.py:24
  133.4 0.9 copy.63
  134.3 1.9 %collective-permute-start.4 = (bf16[128,1024]{1,0:T(8,128)(2,1)}, bf16[128,1024]{1,0:T(8,128)(2,1)}, u32[]{:S(2)}, u32[]{:S(2)}) collective-permute-start(bf16[128,1024]{1,0:T(8,128)(2,1)} %copy.63), channel_id=1, source_target_pairs={{2,0},{3,1},{4,2},{5,3},{6,4},{7,5},{8,6},{9,7},{10,8},{11,9},{12,... | collective-permute-start | bytes 786440 | tf_op jit(solution)/shard_map/ppermute | solution.py:24
  136.2 0.8 fusion.18
  137.0 1.1 copy.69
  138.1 1.9 %collective-permute-start.7 = (bf16[128,1024]{1,0:T(8,128)(2,1)S(1)}, bf16[128,1024]{1,0:T(8,128)(2,1)S(1)}, u32[]{:S(2)}, u32[]{:S(2)}) collective-permute-start(bf16[128,1024]{1,0:T(8,128)(2,1)S(1)} %copy.69), channel_id=1, source_target_pairs={{1,0},{2,1},{3,2},{4,3},{5,4},{6,5},{7,6},{8,7},{9,8},{10,9},{11,1... | collective-permute-start | bytes 786440 | tf_op jit(solution)/shard_map/ppermute | solution.py:24
  140.1 0.9 copy.67
  140.9 1.9 %collective-permute-start.6 = (bf16[128,1024]{1,0:T(8,128)(2,1)}, bf16[128,1024]{1,0:T(8,128)(2,1)S(1)}, u32[]{:S(2)}, u32[]{:S(2)}) collective-permute-start(bf16[128,1024]{1,0:T(8,128)(2,1)} %copy.67), channel_id=1, source_target_pairs={{2,0},{3,1},{4,2},{5,3},{6,4},{7,5},{8,6},{9,7},{10,8},{11,9},{12,... | collective-permute-start | bytes 786440 | tf_op jit(solution)/shard_map/ppermute | solution.py:24
  143.3 0.9 copy.70
  144.1 1.1 slice.66
  145.4 1.1 slice.69
  146.7 1.9 %add_convert_fusion.1 = bf16[128,1024]{1,0:T(8,128)(2,1)} fusion(bf16[128,1024]{1,0:T(8,128)(2,1)} %collective-permute-done.5, f32[128,1024]{1,0:T(8,128)S(1)} %copy.64, bf16[128,1024]{1,0:T(8,128)(2,1)} %collective-permute-done.4), kind=kLoop, calls=%fused_computation.20 | loop fusion | flops 655360 | bytes 1310720 | tf_op jit(solution)/shard_map/convert_element_type | solution.py:423
  148.6 5.9 %collective-permute-done.6 = bf16[128,1024]{1,0:T(8,128)(2,1)S(1)} collective-permute-done((bf16[128,1024]{1,0:T(8,128)(2,1)}, bf16[128,1024]{1,0:T(8,128)(2,1)S(1)}, u32[]{:S(2)}, u32[]{:S(2)}) %collective-permute-start.6) | collective-permute-done | bytes 262176 | tf_op jit(solution)/shard_map/ppermute | solution.py:24
  156.0 4.9 %copy.81 = f32[1,1024,1024]{2,1,0:T(8,128)} copy(f32[1,1024,1024]{2,1,0:T(8,128)} %bitcast.70) | data formatting | bytes 8388608
  160.9 2.1 %copy.82 = f32[1,1024,1024]{2,1,0:T(8,128)} copy(f32[1,1024,1024]{2,1,0:T(8,128)S(1)} %bitcast.69) | data formatting | bytes 8388608
  163.1 1.6 copy-done
  164.6 2.0 %copy.83 = f32[1,1024,1024]{2,1,0:T(8,128)} copy(f32[1,1024,1024]{2,1,0:T(8,128)S(1)} %bitcast.68) | data formatting | bytes 8388608
  (51 shorter events, 9.7 us)
Async XLA Ops:
  0.6 115.9 %collective-permute-start.1 = (bf16[128,1024]{1,0:T(8,128)(2,1)}, bf16[128,1024]{1,0:T(8,128)(2,1)S(1)}, u32[]{:S(2)}, u32[]{:S(2)}) collective-permute-start(bf16[128,1024]{1,0:T(8,128)(2,1)} %param.12), channel_id=1, source_target_pairs={{0,1},{1,2},{2,3},{3,4},{4,5},{5,6},{6,7},{7,8},{8,9},{9,10},{10,1... | collective-permute-start | bytes 786440 | tf_op jit(solution)/shard_map/ppermute | solution.py:24
  2.6 114.0 %collective-permute-start = (bf16[128,1024]{1,0:T(8,128)(2,1)}, bf16[128,1024]{1,0:T(8,128)(2,1)S(1)}, u32[]{:S(2)}, u32[]{:S(2)}) collective-permute-start(bf16[128,1024]{1,0:T(8,128)(2,1)} %param.12), channel_id=1, source_target_pairs={{0,2},{1,3},{2,4},{3,5},{4,6},{5,7},{6,8},{7,9},{8,10},{9,11},{10,... | collective-permute-start | bytes 786440 | tf_op jit(solution)/shard_map/ppermute | solution.py:24
  6.0 111.8 %collective-permute-start.3 = (bf16[128,1024]{1,0:T(8,128)(2,1)}, bf16[128,1024]{1,0:T(8,128)(2,1)S(1)}, u32[]{:S(2)}, u32[]{:S(2)}) collective-permute-start(bf16[128,1024]{1,0:T(8,128)(2,1)} %param.13), channel_id=1, source_target_pairs={{0,1},{1,2},{2,3},{3,4},{4,5},{5,6},{6,7},{7,8},{8,9},{9,10},{10,1... | collective-permute-start | bytes 786440 | tf_op jit(solution)/shard_map/ppermute | solution.py:24
  9.2 108.6 %collective-permute-start.2 = (bf16[128,1024]{1,0:T(8,128)(2,1)}, bf16[128,1024]{1,0:T(8,128)(2,1)S(1)}, u32[]{:S(2)}, u32[]{:S(2)}) collective-permute-start(bf16[128,1024]{1,0:T(8,128)(2,1)} %param.13), channel_id=1, source_target_pairs={{0,2},{1,3},{2,4},{3,5},{4,6},{5,7},{6,8},{7,9},{8,10},{9,11},{10,... | collective-permute-start | bytes 786440 | tf_op jit(solution)/shard_map/ppermute | solution.py:24
  17.7 97.8 %copy-start.8 = (bf16[128,1024]{1,0:T(8,128)(2,1)S(1)}, bf16[128,1024]{1,0:T(8,128)(2,1)}, u32[]{:S(2)}) copy-start(bf16[128,1024]{1,0:T(8,128)(2,1)} %param.11) | copy-start | bytes 786436
  17.7 98.8 %copy-start.9 = (bf16[128,1024]{1,0:T(8,128)(2,1)S(1)}, bf16[128,1024]{1,0:T(8,128)(2,1)}, u32[]{:S(2)}) copy-start(bf16[128,1024]{1,0:T(8,128)(2,1)} %param.12) | copy-start | bytes 786436
  116.5 1.3 copy-start.10
  121.5 1.7 %copy-start.2 = (f32[16,128,384]{1,2,0:T(8,128)}, f32[16,128,384]{1,2,0:T(8,128)S(1)}, u32[]{:S(2)}) copy-start(f32[16,128,384]{1,2,0:T(8,128)S(1)} %get-tuple-element.49) | copy-start | bytes 9437188
  123.2 2.0 %copy-start.5 = (bf16[384,1024]{0,1:T(8,128)(2,1)S(1)}, bf16[384,1024]{0,1:T(8,128)(2,1)}, u32[]{:S(2)}) copy-start(bf16[384,1024]{0,1:T(8,128)(2,1)} %copy.58) | copy-start | bytes 2359300
  123.2 2.7 %copy-start.3 = (f32[16,128,384]{1,2,0:T(8,128)S(1)}, f32[16,128,384]{1,2,0:T(8,128)}, u32[]{:S(2)}) copy-start(f32[16,128,384]{1,2,0:T(8,128)} %copy-done.2) | copy-start | bytes 9437188
  125.9 0.9 copy-start.6
  129.6 13.2 %copy-start.4 = (bf16[384,1024]{0,1:T(8,128)(2,1)S(1)}, bf16[384,1024]{0,1:T(8,128)(2,1)}, u32[]{:S(2)}) copy-start(bf16[384,1024]{0,1:T(8,128)(2,1)} %copy.54) | copy-start | bytes 2359300
  131.5 15.2 %collective-permute-start.5 = (bf16[128,1024]{1,0:T(8,128)(2,1)}, bf16[128,1024]{1,0:T(8,128)(2,1)}, u32[]{:S(2)}, u32[]{:S(2)}) collective-permute-start(bf16[128,1024]{1,0:T(8,128)(2,1)} %copy.65), channel_id=1, source_target_pairs={{1,0},{2,1},{3,2},{4,3},{5,4},{6,5},{7,6},{8,7},{9,8},{10,9},{11,1... | collective-permute-start | bytes 786440 | tf_op jit(solution)/shard_map/ppermute | solution.py:24
  134.3 12.5 %collective-permute-start.4 = (bf16[128,1024]{1,0:T(8,128)(2,1)}, bf16[128,1024]{1,0:T(8,128)(2,1)}, u32[]{:S(2)}, u32[]{:S(2)}) collective-permute-start(bf16[128,1024]{1,0:T(8,128)(2,1)} %copy.63), channel_id=1, source_target_pairs={{2,0},{3,1},{4,2},{5,3},{6,4},{7,5},{8,6},{9,7},{10,8},{11,9},{12,... | collective-permute-start | bytes 786440 | tf_op jit(solution)/shard_map/ppermute | solution.py:24
  138.1 10.5 %collective-permute-start.7 = (bf16[128,1024]{1,0:T(8,128)(2,1)S(1)}, bf16[128,1024]{1,0:T(8,128)(2,1)S(1)}, u32[]{:S(2)}, u32[]{:S(2)}) collective-permute-start(bf16[128,1024]{1,0:T(8,128)(2,1)S(1)} %copy.69), channel_id=1, source_target_pairs={{1,0},{2,1},{3,2},{4,3},{5,4},{6,5},{7,6},{8,7},{9,8},{10,9},{11,1... | collective-permute-start | bytes 786440 | tf_op jit(solution)/shard_map/ppermute | solution.py:24
  140.9 13.5 %collective-permute-start.6 = (bf16[128,1024]{1,0:T(8,128)(2,1)}, bf16[128,1024]{1,0:T(8,128)(2,1)S(1)}, u32[]{:S(2)}, u32[]{:S(2)}) collective-permute-start(bf16[128,1024]{1,0:T(8,128)(2,1)} %copy.67), channel_id=1, source_target_pairs={{2,0},{3,1},{4,2},{5,3},{6,4},{7,5},{8,6},{9,7},{10,8},{11,9},{12,... | collective-permute-start | bytes 786440 | tf_op jit(solution)/shard_map/ppermute | solution.py:24
  146.7 8.6 %copy-start.7 = (bf16[128,1024]{1,0:T(8,128)(2,1)S(1)}, bf16[128,1024]{1,0:T(8,128)(2,1)}, u32[]{:S(2)}) copy-start(bf16[128,1024]{1,0:T(8,128)(2,1)} %get-tuple-element.68) | copy-start | bytes 786436
  156.0 4.9 %copy-start.1 = (f32[1024,1024]{1,0:T(8,128)S(1)}, f32[1024,1024]{1,0:T(8,128)}, u32[]{:S(2)}) copy-start(f32[1024,1024]{1,0:T(8,128)} %get-tuple-element.13) | copy-start | bytes 12582916
  160.9 3.7 %copy-start = (f32[1024,1024]{1,0:T(8,128)S(1)}, f32[1024,1024]{1,0:T(8,128)}, u32[]{:S(2)}) copy-start(f32[1024,1024]{1,0:T(8,128)} %get-tuple-element.14) | copy-start | bytes 12582916
where the time goes:
time: 167 us
  Pallas kernels  96.6 us (58%)
  local copies, waits for them, and re-layouts  29.6 us (18%)
  starting transfers between devices  19.6 us (12%)
  matrix products  8.2 us (5%)
  waiting for transfers between devices  5.87 us (4%)
  other arithmetic  5.83 us (3%)
    pallas_call x1, Pallas kernels, expert_part(): pl.pallas_call(functools.partial(expert_kernel, n, cap), out_shape=(jax.S...  96.6 us
    ppermute x8, starting transfers between devices, shifted(): return lax.ppermute(block, axis, route)  19.6 us
    unnamed x28, local copies, waits for them, and re-layouts  14.8 us
    ppermute x8, waiting for transfers between devices, shifted(): return lax.ppermute(block, axis, route)  5.87 us
  transfers between devices with their start and end apart: 8, of which 1 were waited for; matrix products, arithmetic and copies ran while one was open for 11% of the time, Pallas kernels for 58%

commit v1 on v0

v1 whole, which is shorter than its diff:
```python
import functools
import math

import jax
import jax.numpy as jnp
from jax import lax
from jax.experimental import pallas as pl
from jax.experimental.pallas import tpu as pltpu
from jax.sharding import PartitionSpec as P

D = 1024
HEADS = 16
HEAD = 64
SPAN = 64
LEFT = 256


EPSILON = 1e-06


MESH = pl.DeviceIdType.MESH
CHUNKS = 4
TILE = 256


def nt(a, b):
    return lax.dot_general(a, b, (((1,), (1,)), ((), ())), preferred_element_type=jnp.float32)


def tn(a, b):
    return lax.dot_general(a, b, (((0,), (0,)), ((), ())), preferred_element_type=jnp.float32)


def expert_kernel(
    n, cap,
    route_ref, q_ref, k_ref, v_ref, stream_ref, grad_ref, gain_ref, wg_hbm, wu_hbm, wd_hbm,
    gq_ref, gk_ref, gv_ref, sgrad_ref, gg_hbm, ug_hbm, dg_hbm,
    pick, norm_s, send, kv, halo_out, halo_in, own, xg, wg, wu, wd, acted, dgate, dup, part, from_core, from_x, back, grads,
    w_sem, out_sem, loc_sem, d_send, d_recv, a_send, a_recv, b_send, b_recv, c_send, c_recv,
    kv_send, kv_recv, h_send, h_recv,
):
    i = lax.axis_index("tm")
    j = lax.axis_index("ep")
    j1 = j + 1 - 2 * (j % 2)
    j2 = (j + 2) % 4
    j3 = (j1 + 2) % 4
    width = stream_ref.shape[1]
    hidden = wg.shape[1]
    frames = stream_ref.shape[0]
    per = n // CHUNKS
    rows = per * 4 * cap

    weights = [
        pltpu.make_async_copy(src, dst, w_sem.at[q])
        for q, (src, dst) in enumerate(((wg_hbm, wg), (wu_hbm, wu), (wd_hbm, wd)))
    ]
    for copy in weights:
        copy.start()

    place = i * 4 + j
    places = n * 4

    def at(q):
        return (q // 4, q % 4)

    def nearby(act):
        for away in (1, 2):
            pl.when(place + away < places)(functools.partial(act, place + away))
            pl.when(place >= away)(functools.partial(act, place - away))

    barrier = pltpu.get_barrier_semaphore()
    nearby(lambda q: pl.semaphore_signal(barrier, inc=1, device_id=at(q), device_id_type=MESH))
    for d in range(1, n):
        pl.semaphore_signal(barrier, inc=1, device_id=((i + d) % n, j), device_id_type=MESH)
    pl.semaphore_signal(barrier, inc=1, device_id=(i, j1), device_id_type=MESH)
    pl.semaphore_signal(barrier, inc=1, device_id=(i, j2), device_id_type=MESH)

    stream_f = stream_ref[...].astype(jnp.float32)
    inverse_rms = lax.rsqrt(jnp.mean(stream_f * stream_f, -1, keepdims=True) + EPSILON)
    norm_s[...] = (stream_f * inverse_rms * gain_ref[...]).astype(jnp.bfloat16)

    kv[0, 2] = k_ref[...]
    kv[1, 2] = v_ref[...]

    names = lax.broadcasted_iota(jnp.int32, (n, frames), 0).astype(jnp.float32)
    chosen = [(names == route_ref[h : h + 1, :]).astype(jnp.float32) for h in range(2)]
    first = lax.broadcasted_iota(jnp.int32, (frames, frames), 0)
    second = lax.broadcasted_iota(jnp.int32, (frames, frames), 1)
    earlier = (first < second).astype(jnp.float32).astype(jnp.bfloat16)
    before = jnp.dot(
        (chosen[0] + chosen[1]).astype(jnp.bfloat16), earlier, preferred_element_type=jnp.float32
    )
    row_of = [
        route_ref[h : h + 1, :] * float(cap) + jnp.sum(before * chosen[h], 0, keepdims=True) for h in range(2)
    ]

    ahead = jnp.minimum(places - 1 - place, 2)
    pl.semaphore_wait(barrier, n + 1 + ahead + jnp.minimum(place, 2))

    def remote(src, dst, ssem, rsem, to):
        return pltpu.make_async_remote_copy(
            src_ref=src, dst_ref=dst, send_sem=ssem, recv_sem=rsem, device_id=to, device_id_type=MESH
        )

    def to_expert(d):
        return remote(send.at[d], xg.at[d, j], d_send.at[d, 0], d_recv.at[d, 0], ((i + d) % n, j))

    own_copy = pltpu.make_async_copy(send.at[0], xg.at[0, j], loc_sem)
    for d in list(range(1, n)) + [0]:
        e = (i + d) % n
        row_ids = (lax.broadcasted_iota(jnp.int32, (cap, frames), 0) + e * cap).astype(jnp.float32)
        hits = [(row_ids == row_of[h]).astype(jnp.float32) for h in range(2)]
        chance = sum(jnp.sum(hits[h] * route_ref[2 + h : 3 + h, :], 1, keepdims=True) for h in range(2))
        choice = (hits[0] + hits[1]).astype(jnp.bfloat16)
        pick[e] = choice
        send[d, 0] = jnp.dot(choice, norm_s[...], preferred_element_type=jnp.float32).astype(jnp.bfloat16)
        grad_rows = jnp.dot(choice, grad_ref[...], preferred_element_type=jnp.float32)
        send[d, 1] = (grad_rows * chance).astype(jnp.bfloat16)
        if d:
            to_expert(d).start()
        else:
            own_copy.start()

    even = j % 2 == 0

    def kv_all(away):
        return [
            remote(
                kv.at[q, 2], kv.at[q, 2 - away], kv_send.at[q, away], kv_recv.at[q, 2 - away], at(place + away)
            )
            for q in range(2)
        ]

    def kv_forwards():
        return [
            remote(kv.at[q, 1], kv.at[q, 0], kv_send.at[q, 0], kv_recv.at[q, 0], at(place + 1))
            for q in range(2)
        ]

    def each(copies, what):
        for copy in copies:
            getattr(copy, what)()

    has_next = place + 1 < places
    has_second = place + 2 < places

    @pl.when(has_next)
    def _():
        each(kv_all(1), "start")

    @pl.when(jnp.logical_and(even, has_second))
    def _():
        each(kv_all(2), "start")

    def kv_forward():
        @pl.when(place >= 1)
        def _():
            each(kv_all(1), "wait_recv")

        @pl.when(place < 1)
        def _():
            kv[:, 1] = jnp.zeros_like(kv[:, 1])

        @pl.when(jnp.logical_and(even, place >= 1))
        def _():
            each(kv_forwards(), "start")

    def kv_finish():
        @pl.when(place >= 2)
        def _():
            each(kv_all(2), "wait_recv")

        @pl.when(place < 2)
        def _():
            kv[:, 0] = jnp.zeros_like(kv[:, 0])

    scale = 1.0 / math.sqrt(HEAD)
    lane = lax.broadcasted_iota(jnp.int32, (1, 2 * HEAD), 1)
    low = (lane < HEAD).astype(jnp.float32).astype(jnp.bfloat16)
    high = (lane >= HEAD).astype(jnp.float32).astype(jnp.bfloat16)
    reach = LEFT + frames

    def paired(block):
        return jnp.concatenate([block * low, block * high], 0)

    def pair_columns(t):
        return pl.ds(pl.multiple_of(t * 2 * HEAD, 2 * HEAD), 2 * HEAD)

    def attend(begin, stop):
        row = lax.broadcasted_iota(jnp.int32, (2 * frames, reach), 0)
        col = lax.broadcasted_iota(jnp.int32, (2 * frames, reach), 1)
        start = (row % frames) // SPAN * SPAN
        seen = jnp.logical_and(col >= start, col < start + SPAN + LEFT)
        seen = jnp.logical_and(seen, col >= LEFT - place * frames)

        @pl.loop(begin, stop)
        def _(t):
            cols = pair_columns(t)
            keys = kv[0, :, :, cols].reshape(reach, 2 * HEAD)
            scores = nt(paired(q_ref[:, cols]), keys) * scale
            scores = jnp.where(seen, scores, -jnp.inf)
            exps = jnp.exp(scores - jnp.max(scores, -1, keepdims=True))
            probs = exps / jnp.sum(exps, -1, keepdims=True)
            here = pl.ds(pl.multiple_of(t * frames, frames), frames)
            grads[1, here, 0:reach] = probs[:frames]
            grads[1, here, reach : 2 * reach] = probs[frames:]

    def attend_back():
        @pl.loop(0, width // (2 * HEAD))
        def _(t):
            cols = pair_columns(t)
            here = pl.ds(pl.multiple_of(t * frames, frames), frames)
            keys = kv[0, :, :, cols].reshape(reach, 2 * HEAD)
            vals = kv[1, :, :, cols].reshape(reach, 2 * HEAD)
            probs = jnp.concatenate([grads[1, here, 0:reach], grads[1, here, reach : 2 * reach]], 0)
            pround = probs.astype(jnp.bfloat16)
            outs = paired(sgrad_ref[:, cols])
            dprob = nt(outs, vals)
            row_delta = jnp.sum(pround.astype(jnp.float32) * dprob, -1, keepdims=True)
            dscore = (probs * (dprob - row_delta)).astype(jnp.bfloat16)
            gq = jnp.dot(dscore, keys, preferred_element_type=jnp.float32) * scale
            gq_ref[:, cols] = jnp.where(lane < HEAD, gq[:frames], gq[frames:]).astype(jnp.bfloat16)
            for q, total in ((0, tn(dscore, paired(q_ref[:, cols])) * scale), (1, tn(pround, outs))):
                for piece in range(2):
                    part_rows = total[piece * frames : (piece + 1) * frames]
                    halo_out[piece, q, :, cols] = part_rows.astype(jnp.bfloat16)
                own[q, :, cols] = total[LEFT:]

    def halo_copy(away):
        return remote(
            halo_out.at[2 - away], halo_in.at[2 - away], h_send.at[away - 1], h_recv.at[away - 1], at(place - away)
        )

    def own_to_core(d):
        return remote(xg.at[d, j], xg.at[d, j], d_send.at[d, 1], d_recv.at[d, 1], (i, j1))

    def own_to_x(d):
        return remote(xg.at[d, j], xg.at[d, j], d_send.at[d, 2], d_recv.at[d, 2], (i, j2))

    def x_to_core(d):
        return remote(xg.at[d, j2], xg.at[d, j2], d_send.at[d, 3], d_recv.at[d, 3], (i, j1))

    def span(c):
        return range(c * per, (c + 1) * per)

    def forward_own(c):
        for d in span(c):
            if d:
                to_expert(d).wait_recv()
            else:
                own_copy.wait()
            own_to_x(d).start()
            own_to_core(d).start()

    def forward_x(c):
        for d in span(c):
            own_to_x(d).wait_recv()
            x_to_core(d).start()

    def gather(c):
        for d in span(c):
            own_to_core(d).wait_recv()
            x_to_core(d).wait_recv()

    def compute(c):
        here = pl.ds(c * rows, rows)

        @pl.loop(0, hidden // TILE)
        def _(t):
            cols = pl.ds(pl.multiple_of(t * TILE, TILE), TILE)
            x = xg[c * per : (c + 1) * per, :, 0].reshape(rows, width)
            g = xg[c * per : (c + 1) * per, :, 1].reshape(rows, width)
            gate_pre = jnp.dot(x, wg[:, cols], preferred_element_type=jnp.float32)
            up_pre = jnp.dot(x, wu[:, cols], preferred_element_type=jnp.float32)
            dact = nt(g, wd[cols, :])
            sig = jax.nn.sigmoid(gate_pre)
            silu = gate_pre * sig
            acted[here, cols] = (silu * up_pre).astype(jnp.bfloat16)
            dgate[here, cols] = (dact * up_pre * sig * (1.0 + gate_pre * (1.0 - sig))).astype(jnp.bfloat16)
            dup[here, cols] = (dact * silu).astype(jnp.bfloat16)

        @pl.loop(0, width // TILE)
        def _(t):
            cols = pl.ds(pl.multiple_of(t * TILE, TILE), TILE)
            dx = nt(dgate[here, :], wg[cols, :]) + nt(dup[here, :], wu[cols, :])
            part[c * per : (c + 1) * per, :, :, cols] = dx.astype(jnp.bfloat16).reshape(per, 4, cap, TILE)

    def core_copies(d):
        return (
            remote(part.at[d, j1], from_core.at[d, 0], a_send.at[d, 0], a_recv.at[d, 0], (i, j1)),
            remote(part.at[d, j3], from_core.at[d, 1], a_send.at[d, 1], a_recv.at[d, 1], (i, j1)),
        )

    def x_copy(d):
        return remote(part.at[d, j2], from_x.at[d], b_send.at[d], b_recv.at[d], (i, j2))

    def home_copy(d):
        return remote(part.at[d, j], back.at[i], c_send.at[d], c_recv.at[d], ((i + n - d) % n, j))

    def stage_a(c):
        for d in span(c):
            for copy in core_copies(d):
                copy.start()

    def stage_b(c):
        for d in span(c):
            core_copies(d)[1].wait_recv()
            total = part[d, j2].astype(jnp.float32) + from_core[d, 1].astype(jnp.float32)
            part[d, j2] = total.astype(jnp.bfloat16)
            x_copy(d).start()

    def stage_c(c):
        for d in span(c):
            core_copies(d)[0].wait_recv()
            x_copy(d).wait_recv()
            total = part[d, j].astype(jnp.float32) + from_core[d, 0].astype(jnp.float32)
            total = (total + from_x[d].astype(jnp.float32)).astype(jnp.bfloat16)
            if d:
                part[d, j] = total
                home_copy(d).start()
            else:
                back[i] = total

    forward_own(0)
    for copy in weights:
        copy.wait()
    forward_own(1)
    for c in range(CHUNKS):
        forward_x(c)
        gather(c)
        compute(c)
        stage_a(c)
        if c + 2 < CHUNKS:
            forward_own(c + 2)
        if c >= 1:
            stage_b(c - 1)
        if c >= 2:
            stage_c(c - 2)
        if c == 1:
            kv_forward()
    kv_finish()
    pairs = width // (2 * HEAD)
    attend(0, pairs // 2)
    stage_b(CHUNKS - 1)
    stage_c(CHUNKS - 2)
    attend(pairs // 2, pairs)
    stage_c(CHUNKS - 1)

    total_rows = n * 4 * cap
    writes = [
        pltpu.make_async_copy(grads.at[q % 2], dst, out_sem.at[q])
        for q, dst in enumerate((dg_hbm, gg_hbm, ug_hbm))
    ]

    @pl.loop(0, hidden // TILE)
    def _(t):
        cols = pl.ds(pl.multiple_of(t * TILE, TILE), TILE)
        lhs = acted[:, cols]
        for q in range(0, width, 512):
            rhs = xg[:, :, 1, :, q : q + 512].reshape(total_rows, 512)
            grads[0, cols, q : q + 512] = tn(lhs, rhs)

    writes[0].start()
    for d in range(1, n):
        home_copy(d).wait_recv()
    dnormed = tn(pick[...].reshape(n * cap, frames), back[...].reshape(n * cap, width))
    stream_f = stream_ref[...].astype(jnp.float32)
    inverse_rms = lax.rsqrt(jnp.mean(stream_f * stream_f, -1, keepdims=True) + EPSILON)
    scaled = stream_f * inverse_rms
    weighted = dnormed * gain_ref[...]
    dstream = inverse_rms * (weighted - scaled * jnp.mean(weighted * scaled, -1, keepdims=True))
    sgrad_ref[...] = (grad_ref[...].astype(jnp.float32) + dstream).astype(jnp.bfloat16)

    attend_back()
    for away in (1, 2):
        @pl.when(place >= away)
        def _():
            halo_copy(away).start()

    writes[0].wait()

    @pl.loop(0, width // TILE)
    def _(t):
        cols = pl.ds(pl.multiple_of(t * TILE, TILE), TILE)
        lhs = xg[:, :, 0, :, cols].reshape(total_rows, TILE)
        for q in range(0, hidden, 512):
            grads[1, cols, q : q + 512] = tn(lhs, dgate[:, q : q + 512])
            grads[0, cols, q : q + 512] = tn(lhs, dup[:, q : q + 512])

    writes[1].start()
    writes[2].start()

    for away in (1, 2):
        @pl.when(place + away < places)
        def _():
            halo_copy(away).wait_recv()

        @pl.when(place + away >= places)
        def _():
            halo_in[2 - away] = jnp.zeros_like(halo_in[2 - away])

    for q, out_ref in ((0, gk_ref), (1, gv_ref)):
        total = own[q] + halo_in[0, q].astype(jnp.float32) + halo_in[1, q].astype(jnp.float32)
        out_ref[...] = total.astype(jnp.bfloat16)

    for away in (1, 2):
        @pl.when(place >= away)
        def _():
            halo_copy(away).wait_send()

    @pl.when(has_next)
    def _():
        each(kv_all(1), "wait_send")

    @pl.when(jnp.logical_and(even, has_second))
    def _():
        each(kv_all(2), "wait_send")

    @pl.when(jnp.logical_and(even, place >= 1))
    def _():
        each(kv_forwards(), "wait_send")

    for d in range(n):
        if d:
            to_expert(d).wait_send()
            home_copy(d).wait_send()
        own_to_core(d).wait_send()
        own_to_x(d).wait_send()
        x_to_core(d).wait_send()
        for copy in core_copies(d):
            copy.wait_send()
        x_copy(d).wait_send()
    for copy in writes[1:]:
        copy.wait()


def expert_part(n, cap, route, queries, keys, values, stream, grad_out, gain, w_gate, w_up, w_down):
    frames, width = stream.shape
    hidden = w_gate.shape[1]
    total = n * 4 * cap
    bf, f32 = jnp.bfloat16, jnp.float32
    vmem = pl.BlockSpec(memory_space=pltpu.VMEM)
    hbm = pl.BlockSpec(memory_space=pl.ANY)
    dma = pltpu.SemaphoreType.DMA
    return pl.pallas_call(
        functools.partial(expert_kernel, n, cap),
        out_shape=(
            jax.ShapeDtypeStruct((frames, width), bf),
            jax.ShapeDtypeStruct((frames, width), bf),
            jax.ShapeDtypeStruct((frames, width), bf),
            jax.ShapeDtypeStruct((frames, width), bf),
            jax.ShapeDtypeStruct((width, hidden), f32),
            jax.ShapeDtypeStruct((width, hidden), f32),
            jax.ShapeDtypeStruct((hidden, width), f32),
        ),
        in_specs=[vmem] * 7 + [hbm] * 3,
        out_specs=(vmem, vmem, vmem, vmem, hbm, hbm, hbm),
        scratch_shapes=[
            pltpu.VMEM((n, cap, frames), bf),
            pltpu.VMEM((frames, width), bf),
            pltpu.VMEM((n, 2, cap, width), bf),
            pltpu.VMEM((2, 3, frames, width), bf),
            pltpu.VMEM((2, 2, frames, width), bf),
            pltpu.VMEM((2, 2, frames, width), bf),
            pltpu.VMEM((2, frames, width), f32),
            pltpu.VMEM((n, 4, 2, cap, width), bf),
            pltpu.VMEM((width, hidden), bf),
            pltpu.VMEM((width, hidden), bf),
            pltpu.VMEM((hidden, width), bf),
            pltpu.VMEM((total, hidden), bf),
            pltpu.VMEM((total, hidden), bf),
            pltpu.VMEM((total, hidden), bf),
            pltpu.VMEM((n, 4, cap, width), bf),
            pltpu.VMEM((n, 2, cap, width), bf),
            pltpu.VMEM((n, cap, width), bf),
            pltpu.VMEM((n, cap, width), bf),
            pltpu.VMEM((2, width, hidden), f32),
            dma((3,)),
            dma((3,)),
            dma,
            dma((n, 4)),
            dma((n, 4)),
            dma((n, 2)),
            dma((n, 2)),
            dma((n,)),
            dma((n,)),
            dma((n,)),
            dma((n,)),
            dma((2, 3)),
            dma((2, 2)),
            dma((2,)),
            dma((2,)),
        ],
        compiler_params=pltpu.CompilerParams(
            collective_id=0, has_side_effects=True, vmem_limit_bytes=60 * 1024 * 1024
        ),
        cost_estimate=pl.CostEstimate(
            flops=16 * total * width * hidden, bytes_accessed=20 * width * hidden, transcendentals=0
        ),
    )(route, queries, keys, values, stream, grad_out, gain, w_gate, w_up, w_down)


def body(
    queries, keys, values, stream, grad_out, norm_gain, gate_probs, routes, w_gate, w_up, w_down
):
    frames = queries.shape[0]
    experts = lax.axis_size("tm")
    capacity = 3 * frames * routes.shape[1] // (2 * experts)
    cap = -(-capacity // 16) * 16
    route = jnp.concatenate([routes.astype(jnp.float32).T, gate_probs.T], 0)
    grad_q, grad_k, grad_v, stream_grad, gate_grad, up_grad, down_grad = expert_part(
        experts, cap, route, queries, keys, values, stream, grad_out, norm_gain[None, :],
        w_gate[0], w_up[0], w_down[0],
    )
    return (
        grad_q, grad_k, grad_v, stream_grad, gate_grad[None], up_grad[None], down_grad[None]
    )


def solution(mesh):
    return jax.shard_map(
        body,
        mesh=mesh,
        in_specs=(
            P(("tm", "ep"), None),
            P(("tm", "ep"), None),
            P(("tm", "ep"), None),
            P(("tm", "ep"), None),
            P(("tm", "ep"), None),
            P(),
            P(("tm", "ep"), None),
            P(("tm", "ep"), None),
            P("tm", None, "ep"),
            P("tm", None, "ep"),
            P("tm", "ep", None),
        ),
        out_specs=(
            P(("tm", "ep"), None),
            P(("tm", "ep"), None),
            P(("tm", "ep"), None),
            P(("tm", "ep"), None),
            P("tm", None, "ep"),
            P("tm", None, "ep"),
            P("tm", "ep", None),
        ),
        check_vma=False,
    )
```

time: 167 us -> 144 us (0.86)
  Pallas kernels: 96.6 us -> 122 us
  starting transfers between devices: 19.6 us -> 0 us
  local copies, waits for them, and re-layouts: 29.6 us -> 17.3 us
  matrix products: 8.2 us -> 0 us
  waiting for transfers between devices: 5.87 us -> 0 us
  other arithmetic: 5.83 us -> 1.94 us
    pallas_call x1, Pallas kernels: 96.6 us -> 122 us  [expert_part(): pl.pallas_call(functools.partial(expert_kernel, n, cap), out_shape=(jax.S...]
    ppermute x8 -> x0, starting transfers between devices: 19.6 us -> none  [shifted(): return lax.ppermute(block, axis, route)]
    ppermute x8 -> x0, waiting for transfers between devices: 5.87 us -> none  [shifted(): return lax.ppermute(block, axis, route)]
    dot_general x6 -> x0, matrix products: 5.77 us -> none  [the longest x1 1.97 us: attend_grads(): jnp.einsum('hqk,qhd->khd', dscore, q_three, preferred_element_type=jnp.fl...]
    convert_element_type x4 -> x0, local copies, waits for them, and re-layouts: 4.67 us -> none  [the longest x2 2.71 us: body(): padded_k[offset_index * frames:(offset_index + 1) * frames]]
    convert_element_type x5 -> x0, other arithmetic: 4.55 us -> none  [the longest x1 1.87 us: body(): keys_total.astype(jnp.bfloat16)]
    slice x6 -> x0, local copies, waits for them, and re-layouts: 4.24 us -> none  [the longest x2 1.28 us: body(): values_total = grad_v[LEFT:]]
    unnamed x28 -> x11, local copies, waits for them, and re-layouts: 14.8 us -> 17.3 us
  transfers between devices with their start and end apart: 8 -> 0, of which waited for: 1 -> 0; matrix products, arithmetic and copies ran while one was open for 11% -> 0% of each run, Pallas kernels for 58% -> 0%
where the time goes in v1:
time: 144 us; the launch traced here: 142 us
  Pallas kernels  122 us (85%)
  local copies, waits for them, and re-layouts  17.3 us (12%)
  other arithmetic  1.94 us (1%)
    pallas_call x1, Pallas kernels, expert_part(): pl.pallas_call(functools.partial(expert_kernel, n, cap), out_shape=(jax.S...  122 us
    unnamed x11, local copies, waits for them, and re-layouts  17.3 us

profile of v1, /device:TPU:24, one launch (start us, length us, event | category | flops | bytes accessed | tf_op | source)
XLA Modules:
  0.0 142.2 jit_solution(1999000460781804085)
XLA Ops:
  0.6 0.7 convert_bitcast_fusion
  1.3 1.3 pad_maximum_fusion.route_ref
  2.6 122.3 %shard_map.162 = (bf16[128,1024]{1,0:T(8,128)(2,1)}, bf16[128,1024]{1,0:T(8,128)(2,1)}, bf16[128,1024]{1,0:T(8,128)(2,1)}, bf16[128,1024]{1,0:T(8,128)(2,1)}, f3...) custom-call(f32[4,128]{1,0:T(4,128)} %pad_maximum_fusion.route_ref, bf16[128,1024]{1,0:T(8,128)(2,1)} %q_ref.1, ...), custom_call_target="tpu_custom_call" | custom-call | flops 25769803776 | bytes 20971520 | tf_op jit(solution)/shard_map/pallas_call | solution.py:445
  124.8 1.7 %copy.25 = bf16[128,1024]{1,0:T(8,128)(2,1)} copy(bf16[128,1024]{1,0:T(8,128)(2,1)} %get-tuple-element.28) | data formatting | bytes 524288
  126.5 1.7 %copy.26 = bf16[128,1024]{1,0:T(8,128)(2,1)} copy(bf16[128,1024]{1,0:T(8,128)(2,1)} %get-tuple-element.29) | data formatting | bytes 524288
  128.2 1.7 %copy.27 = bf16[128,1024]{1,0:T(8,128)(2,1)} copy(bf16[128,1024]{1,0:T(8,128)(2,1)} %get-tuple-element.30) | data formatting | bytes 524288
  129.9 1.7 %copy.28 = bf16[128,1024]{1,0:T(8,128)(2,1)} copy(bf16[128,1024]{1,0:T(8,128)(2,1)} %get-tuple-element.31) | data formatting | bytes 524288
  131.5 0.0 copy-start.1
  131.5 4.9 %copy.29 = f32[1,1024,1024]{2,1,0:T(8,128)} copy(f32[1,1024,1024]{2,1,0:T(8,128)} %bitcast.12) | data formatting | bytes 8388608
  136.5 0.0 copy-done.1
  136.5 0.0 copy-start
  136.5 2.1 %copy.30 = f32[1,1024,1024]{2,1,0:T(8,128)} copy(f32[1,1024,1024]{2,1,0:T(8,128)S(1)} %bitcast.11) | data formatting | bytes 8388608
  138.6 1.6 %copy-done = f32[1024,1024]{1,0:T(8,128)S(1)} copy-done((f32[1024,1024]{1,0:T(8,128)S(1)}, f32[1024,1024]{1,0:T(8,128)}, u32[]{:S(2)}) %copy-start) | copy-done | bytes 4194328
  140.2 2.0 %copy.31 = f32[1,1024,1024]{2,1,0:T(8,128)} copy(f32[1,1024,1024]{2,1,0:T(8,128)S(1)} %bitcast.10) | data formatting | bytes 8388608
Async XLA Ops:
  131.5 4.9 %copy-start.1 = (f32[1024,1024]{1,0:T(8,128)S(1)}, f32[1024,1024]{1,0:T(8,128)}, u32[]{:S(2)}) copy-start(f32[1024,1024]{1,0:T(8,128)} %get-tuple-element.19) | copy-start | bytes 12582916
  136.5 3.7 %copy-start = (f32[1024,1024]{1,0:T(8,128)S(1)}, f32[1024,1024]{1,0:T(8,128)}, u32[]{:S(2)}) copy-start(f32[1024,1024]{1,0:T(8,128)} %get-tuple-element.20) | copy-start | bytes 12582916

commit v2 on v1

--- a/solution.py
+++ b/solution.py
@@ -34,8 +34,8 @@
 def expert_kernel(
     n, cap,
     route_ref, q_ref, k_ref, v_ref, stream_ref, grad_ref, gain_ref, wg_hbm, wu_hbm, wd_hbm,
-    gq_ref, gk_ref, gv_ref, sgrad_ref, gg_hbm, ug_hbm, dg_hbm,
-    pick, norm_s, send, kv, halo_out, halo_in, own, xg, wg, wu, wd, acted, dgate, dup, part, from_core, from_x, back, grads,
+    gq_ref, gk_ref, gv_ref, sgrad_ref, gg_hbm, dg_hbm, x_hbm, dup_hbm,
+    pick, norm_s, send, kv, halo_out, halo_in, own, kept, xg, wg, wu, wd, acted, dgate, dup, part, from_core, from_x, back, grads,
     w_sem, out_sem, loc_sem, d_send, d_recv, a_send, a_recv, b_send, b_recv, c_send, c_recv,
     kv_send, kv_recv, h_send, h_recv,
 ):
@@ -104,6 +104,37 @@
 
     def to_expert(d):
         return remote(send.at[d], xg.at[d, j], d_send.at[d, 0], d_recv.at[d, 0], ((i + d) % n, j))
+
+    even = j % 2 == 0
+
+    def kv_all(away):
+        return [
+            remote(
+                kv.at[q, 2], kv.at[q, 2 - away], kv_send.at[q, away], kv_recv.at[q, 2 - away], at(place + away)
+            )
+            for q in range(2)
+        ]
+
+    def kv_forwards():
+        return [
+            remote(kv.at[q, 1], kv.at[q, 0], kv_send.at[q, 0], kv_recv.at[q, 0], at(place + 1))
+            for q in range(2)
+        ]
+
+    def each(copies, what):
+        for copy in copies:
+            getattr(copy, what)()
+
+    has_next = place + 1 < places
+    has_second = place + 2 < places
+
+    @pl.when(has_next)
+    def _():
+        each(kv_all(1), "start")
+
+    @pl.when(jnp.logical_and(even, has_second))
+    def _():
+        each(kv_all(2), "start")
 
     own_copy = pltpu.make_async_copy(send.at[0], xg.at[0, j], loc_sem)
     for d in list(range(1, n)) + [0]:
@@ -121,37 +152,6 @@
         else:
             own_copy.start()
 
-    even = j % 2 == 0
-
-    def kv_all(away):
-        return [
-            remote(
-                kv.at[q, 2], kv.at[q, 2 - away], kv_send.at[q, away], kv_recv.at[q, 2 - away], at(place + away)
-            )
-            for q in range(2)
-        ]
-
-    def kv_forwards():
-        return [
-            remote(kv.at[q, 1], kv.at[q, 0], kv_send.at[q, 0], kv_recv.at[q, 0], at(place + 1))
-            for q in range(2)
-        ]
-
-    def each(copies, what):
-        for copy in copies:
-            getattr(copy, what)()
-
-    has_next = place + 1 < places
-    has_second = place + 2 < places
-
-    @pl.when(has_next)
-    def _():
-        each(kv_all(1), "start")
-
-    @pl.when(jnp.logical_and(even, has_second))
-    def _():
-        each(kv_all(2), "start")
-
     def kv_forward():
         @pl.when(place >= 1)
         def _():
@@ -201,18 +201,15 @@
             scores = jnp.where(seen, scores, -jnp.inf)
             exps = jnp.exp(scores - jnp.max(scores, -1, keepdims=True))
             probs = exps / jnp.sum(exps, -1, keepdims=True)
-            here = pl.ds(pl.multiple_of(t * frames, frames), frames)
-            grads[1, here, 0:reach] = probs[:frames]
-            grads[1, here, reach : 2 * reach] = probs[frames:]
+            kept[t] = probs
 
     def attend_back():
         @pl.loop(0, width // (2 * HEAD))
         def _(t):
             cols = pair_columns(t)
-            here = pl.ds(pl.multiple_of(t * frames, frames), frames)
             keys = kv[0, :, :, cols].reshape(reach, 2 * HEAD)
             vals = kv[1, :, :, cols].reshape(reach, 2 * HEAD)
-            probs = jnp.concatenate([grads[1, here, 0:reach], grads[1, here, reach : 2 * reach]], 0)
+            probs = kept[t]
             pround = probs.astype(jnp.bfloat16)
             outs = paired(sgrad_ref[:, cols])
             dprob = nt(outs, vals)
@@ -321,46 +318,65 @@
             else:
                 back[i] = total
 
+    pairs = width // (2 * HEAD)
     forward_own(0)
-    for copy in weights:
-        copy.wait()
     forward_own(1)
+    kv_forward()
     for c in range(CHUNKS):
         forward_x(c)
+        if c == 0:
+            kv_finish()
+            attend(0, pairs // 2)
+            each(weights, "wait")
+        if c == 1:
+            attend(pairs // 2, pairs)
+        if c >= 1:
+            stage_b(c - 1)
+        if c >= 2:
+            stage_c(c - 2)
         gather(c)
         compute(c)
         stage_a(c)
         if c + 2 < CHUNKS:
             forward_own(c + 2)
-        if c >= 1:
-            stage_b(c - 1)
-        if c >= 2:
-            stage_c(c - 2)
-        if c == 1:
-            kv_forward()
-    kv_finish()
-    pairs = width // (2 * HEAD)
-    attend(0, pairs // 2)
+
+    total_rows = n * 4 * cap
+    writes = [
+        pltpu.make_async_copy(grads.at[0], dg_hbm, out_sem.at[0]),
+        pltpu.make_async_copy(grads.at[1], gg_hbm, out_sem.at[1]),
+        pltpu.make_async_copy(xg.at[:, :, 0], x_hbm, out_sem.at[2]),
+        pltpu.make_async_copy(dup, dup_hbm, out_sem.at[3]),
+    ]
+    writes[2].start()
+    writes[3].start()
+
+    def down_grads(begin, stop):
+        @pl.loop(begin, stop)
+        def _(t):
+            cols = pl.ds(pl.multiple_of(t * TILE, TILE), TILE)
+            lhs = acted[:, cols]
+            for q in range(0, width, 512):
+                rhs = xg[:, :, 1, :, q : q + 512].reshape(total_rows, 512)
+                grads[0, cols, q : q + 512] = tn(lhs, rhs)
+
+    def gate_grads(begin, stop):
+        @pl.loop(begin, stop)
+        def _(t):
+            cols = pl.ds(pl.multiple_of(t * TILE, TILE), TILE)
+            lhs = xg[:, :, 0, :, cols].reshape(total_rows, TILE)
+            for q in range(0, hidden, 512):
+                grads[1, cols, q : q + 512] = tn(lhs, dgate[:, q : q + 512])
+
+    down_tiles = hidden // TILE
+    gate_tiles = width // TILE
+    down_grads(0, down_tiles // 2)
     stage_b(CHUNKS - 1)
     stage_c(CHUNKS - 2)
-    attend(pairs // 2, pairs)
+    down_grads(down_tiles // 2, down_tiles)
+    writes[0].start()
     stage_c(CHUNKS - 1)
-
-    total_rows = n * 4 * cap
-    writes = [
-        pltpu.make_async_copy(grads.at[q % 2], dst, out_sem.at[q])
-        for q, dst in enumerate((dg_hbm, gg_hbm, ug_hbm))
-    ]
-
-    @pl.loop(0, hidden // TILE)
-    def _(t):
-        cols = pl.ds(pl.multiple_of(t * TILE, TILE), TILE)
-        lhs = acted[:, cols]
-        for q in range(0, width, 512):
-            rhs = xg[:, :, 1, :, q : q + 512].reshape(total_rows, 512)
-            grads[0, cols, q : q + 512] = tn(lhs, rhs)
-
-    writes[0].start()
+    gate_grads(0, gate_tiles // 2)
+
     for d in range(1, n):
         home_copy(d).wait_recv()
     dnormed = tn(pick[...].reshape(n * cap, frames), back[...].reshape(n * cap, width))
@@ -377,18 +393,8 @@
         def _():
             halo_copy(away).start()
 
-    writes[0].wait()
-
-    @pl.loop(0, width // TILE)
-    def _(t):
-        cols = pl.ds(pl.multiple_of(t * TILE, TILE), TILE)
-        lhs = xg[:, :, 0, :, cols].reshape(total_rows, TILE)
-        for q in range(0, hidden, 512):
-            grads[1, cols, q : q + 512] = tn(lhs, dgate[:, q : q + 512])
-            grads[0, cols, q : q + 512] = tn(lhs, dup[:, q : q + 512])
-
+    gate_grads(gate_tiles // 2, gate_tiles)
     writes[1].start()
-    writes[2].start()
 
     for away in (1, 2):
         @pl.when(place + away < places)
@@ -430,8 +436,35 @@
         for copy in core_copies(d):
             copy.wait_send()
         x_copy(d).wait_send()
-    for copy in writes[1:]:
-        copy.wait()
+    each(writes, "wait")
+
+
+def finish_kernel(x_ref, dup_ref, *refs):
+    half = len(refs) // 2
+    refs[half][...] = tn(x_ref[...], dup_ref[...])
+    for src, dst in zip(refs[:half], refs[half + 1 :]):
+        dst[...] = src[...]
+
+
+def finish(x_rows, dup_rows, passed):
+    total, width = x_rows.shape
+    hidden = dup_rows.shape[1]
+    steps = width // TILE
+    blocks = [pl.BlockSpec((a.shape[0] // steps, a.shape[1]), lambda t: (t, 0)) for a in passed]
+    up_block = pl.BlockSpec((TILE, hidden), lambda t: (t, 0))
+    return pl.pallas_call(
+        finish_kernel,
+        grid=(steps,),
+        out_shape=[jax.ShapeDtypeStruct((width, hidden), jnp.float32)]
+        + [jax.ShapeDtypeStruct(a.shape, a.dtype) for a in passed],
+        in_specs=[
+            pl.BlockSpec((total, TILE), lambda t: (0, t)),
+            pl.BlockSpec((total, hidden), lambda t: (0, 0)),
+        ]
+        + blocks,
+        out_specs=[up_block] + blocks,
+        compiler_params=pltpu.CompilerParams(vmem_limit_bytes=48 * 1024 * 1024),
+    )(x_rows, dup_rows, *passed)
 
 
 def expert_part(n, cap, route, queries, keys, values, stream, grad_out, gain, w_gate, w_up, w_down):
@@ -450,11 +483,12 @@
             jax.ShapeDtypeStruct((frames, width), bf),
             jax.ShapeDtypeStruct((frames, width), bf),
             jax.ShapeDtypeStruct((width, hidden), f32),
-            jax.ShapeDtypeStruct((width, hidden), f32),
             jax.ShapeDtypeStruct((hidden, width), f32),
+            jax.ShapeDtypeStruct((n, 4, cap, width), bf),
+            jax.ShapeDtypeStruct((total, hidden), bf),
         ),
         in_specs=[vmem] * 7 + [hbm] * 3,
-        out_specs=(vmem, vmem, vmem, vmem, hbm, hbm, hbm),
+        out_specs=(vmem,) * 4 + (hbm,) * 4,
         scratch_shapes=[
             pltpu.VMEM((n, cap, frames), bf),
             pltpu.VMEM((frames, width), bf),
@@ -463,6 +497,7 @@
             pltpu.VMEM((2, 2, frames, width), bf),
             pltpu.VMEM((2, 2, frames, width), bf),
             pltpu.VMEM((2, frames, width), f32),
+            pltpu.VMEM((width // (2 * HEAD), 2 * frames, LEFT + frames), f32),
             pltpu.VMEM((n, 4, 2, cap, width), bf),
             pltpu.VMEM((width, hidden), bf),
             pltpu.VMEM((width, hidden), bf),
@@ -476,7 +511,7 @@
             pltpu.VMEM((n, cap, width), bf),
             pltpu.VMEM((2, width, hidden), f32),
             dma((3,)),
-            dma((3,)),
+            dma((4,)),
             dma,
             dma((n, 4)),
             dma((n, 4)),
@@ -492,7 +527,7 @@
             dma((2,)),
         ],
         compiler_params=pltpu.CompilerParams(
-            collective_id=0, has_side_effects=True, vmem_limit_bytes=60 * 1024 * 1024
+            collective_id=0, has_side_effects=True, vmem_limit_bytes=62 * 1024 * 1024
         ),
         cost_estimate=pl.CostEstimate(
             flops=16 * total * width * hidden, bytes_accessed=20 * width * hidden, transcendentals=0
@@ -508,9 +543,12 @@
     capacity = 3 * frames * routes.shape[1] // (2 * experts)
     cap = -(-capacity // 16) * 16
     route = jnp.concatenate([routes.astype(jnp.float32).T, gate_probs.T], 0)
-    grad_q, grad_k, grad_v, stream_grad, gate_grad, up_grad, down_grad = expert_part(
+    *passed, x_rows, dup_rows = expert_part(
         experts, cap, route, queries, keys, values, stream, grad_out, norm_gain[None, :],
         w_gate[0], w_up[0], w_down[0],
+    )
+    up_grad, grad_q, grad_k, grad_v, stream_grad, gate_grad, down_grad = finish(
+        x_rows.reshape(-1, x_rows.shape[-1]), dup_rows, passed
     )
     return (
         grad_q, grad_k, grad_v, stream_grad, gate_grad[None], up_grad[None], down_grad[None]

time: 144 us -> 157 us (1.090)
  the two profiles are of different devices: /device:TPU:24 before, /device:TPU:0 now
where the time goes in v2:
time: 157 us
  Pallas kernels  148 us (94%)
  local copies, waits for them, and re-layouts  5.68 us (4%)
  other arithmetic  1.94 us (1%)
    pallas_call x1, Pallas kernels, expert_part(): pl.pallas_call(functools.partial(expert_kernel, n, cap), out_shape=(jax.S...  137 us
    pallas_call x1, Pallas kernels, finish(): pl.pallas_call(finish_kernel, grid=(steps,), out_shape=[jax.ShapeDtypeStr...  10.9 us
    unnamed x10, local copies, waits for them, and re-layouts  5.68 us

profile of v2, /device:TPU:0, one launch (start us, length us, event | category | flops | bytes accessed | tf_op | source)
XLA Modules:
  0.0 156.6 jit_solution(11201545300647083808)
XLA Ops:
  0.6 0.7 convert_bitcast_fusion
  1.3 1.3 pad_maximum_fusion.route_ref
  2.6 137.5 %shard_map.162 = (bf16[128,1024]{1,0:T(8,128)(2,1)}, bf16[128,1024]{1,0:T(8,128)(2,1)}, bf16[128,1024]{1,0:T(8,128)(2,1)}, bf16[128,1024]{1,0:T(8,128)(2,1)}, f3...) custom-call(f32[4,128]{1,0:T(4,128)} %pad_maximum_fusion.route_ref, ...), custom_call_target="tpu_custom_call" | custom-call | flops 25769803776 | bytes 20971520 | tf_op jit(solution)/shard_map/pallas_call | solution.py:478
  140.1 0.0 copy-start
  140.1 1.9 %copy-done = bf16[8,4,48,1024]{3,2,1,0:T(8,128)(2,1)S(1)} copy-done((bf16[8,4,48,1024]{3,2,1,0:T(8,128)(2,1)S(1)}, bf16[8,4,48,1024]{3,2,1,0:T(8,128)(2,1)}, u32[]{:S(2)}) %copy-start) | copy-done | bytes 3145752
  141.9 0.0 copy-start.1
  141.9 0.9 copy-done.1
  142.9 0.0 copy-start.2
  142.9 0.9 copy-done.2
  143.8 0.0 copy-start.3
  143.9 0.9 copy-done.3
  144.8 0.0 copy-start.4
  144.8 0.9 copy-done.4
  145.7 10.9 %shard_map.163 = (f32[1024,1024]{1,0:T(8,128)}, bf16[128,1024]{1,0:T(8,128)(2,1)}, bf16[128,1024]{1,0:T(8,128)(2,1)}, bf16[128,1024]{1,0:T(8,128)(2,1)}, bf16[12...) custom-call(bf16[1536,1024]{1,0:T(8,128)(2,1)S(1)} %bitcast.11, ...), custom_call_target="tpu_custom_call" | custom-call | tf_op jit(solution)/shard_map/pallas_call | solution.py:455
Async XLA Ops:
  140.1 1.9 %copy-start = (bf16[8,4,48,1024]{3,2,1,0:T(8,128)(2,1)S(1)}, bf16[8,4,48,1024]{3,2,1,0:T(8,128)(2,1)}, u32[]{:S(2)}) copy-start(bf16[8,4,48,1024]{3,2,1,0:T(8,128)(2,1)} %get-tuple-element.22) | copy-start | bytes 9437188
  141.9 0.9 copy-start.1
  142.9 0.9 copy-start.2
  143.8 0.9 copy-start.3
  144.8 0.9 copy-start.4

commit v3 on v2

--- a/solution.py
+++ b/solution.py
@@ -105,37 +105,6 @@
     def to_expert(d):
         return remote(send.at[d], xg.at[d, j], d_send.at[d, 0], d_recv.at[d, 0], ((i + d) % n, j))
 
-    even = j % 2 == 0
-
-    def kv_all(away):
-        return [
-            remote(
-                kv.at[q, 2], kv.at[q, 2 - away], kv_send.at[q, away], kv_recv.at[q, 2 - away], at(place + away)
-            )
-            for q in range(2)
-        ]
-
-    def kv_forwards():
-        return [
-            remote(kv.at[q, 1], kv.at[q, 0], kv_send.at[q, 0], kv_recv.at[q, 0], at(place + 1))
-            for q in range(2)
-        ]
-
-    def each(copies, what):
-        for copy in copies:
-            getattr(copy, what)()
-
-    has_next = place + 1 < places
-    has_second = place + 2 < places
-
-    @pl.when(has_next)
-    def _():
-        each(kv_all(1), "start")
-
-    @pl.when(jnp.logical_and(even, has_second))
-    def _():
-        each(kv_all(2), "start")
-
     own_copy = pltpu.make_async_copy(send.at[0], xg.at[0, j], loc_sem)
     for d in list(range(1, n)) + [0]:
         e = (i + d) % n
@@ -152,6 +121,37 @@
         else:
             own_copy.start()
 
+    even = j % 2 == 0
+
+    def kv_all(away):
+        return [
+            remote(
+                kv.at[q, 2], kv.at[q, 2 - away], kv_send.at[q, away], kv_recv.at[q, 2 - away], at(place + away)
+            )
+            for q in range(2)
+        ]
+
+    def kv_forwards():
+        return [
+            remote(kv.at[q, 1], kv.at[q, 0], kv_send.at[q, 0], kv_recv.at[q, 0], at(place + 1))
+            for q in range(2)
+        ]
+
+    def each(copies, what):
+        for copy in copies:
+            getattr(copy, what)()
+
+    has_next = place + 1 < places
+    has_second = place + 2 < places
+
+    @pl.when(has_next)
+    def _():
+        each(kv_all(1), "start")
+
+    @pl.when(jnp.logical_and(even, has_second))
+    def _():
+        each(kv_all(2), "start")
+
     def kv_forward():
         @pl.when(place >= 1)
         def _():
@@ -193,7 +193,7 @@
         seen = jnp.logical_and(col >= start, col < start + SPAN + LEFT)
         seen = jnp.logical_and(seen, col >= LEFT - place * frames)
 
-        @pl.loop(begin, stop)
+        @pl.loop(begin, stop, unroll=2)
         def _(t):
             cols = pair_columns(t)
             keys = kv[0, :, :, cols].reshape(reach, 2 * HEAD)
@@ -203,10 +203,13 @@
             probs = exps / jnp.sum(exps, -1, keepdims=True)
             kept[t] = probs
 
-    def attend_back():
-        @pl.loop(0, width // (2 * HEAD))
+    def attend_back(half):
+        begin = half * (width // (4 * HEAD))
+
+        @pl.loop(begin, begin + width // (4 * HEAD), unroll=2)
         def _(t):
             cols = pair_columns(t)
+            half_cols = pair_columns(t - begin)
             keys = kv[0, :, :, cols].reshape(reach, 2 * HEAD)
             vals = kv[1, :, :, cols].reshape(reach, 2 * HEAD)
             probs = kept[t]
@@ -220,12 +223,16 @@
             for q, total in ((0, tn(dscore, paired(q_ref[:, cols])) * scale), (1, tn(pround, outs))):
                 for piece in range(2):
                     part_rows = total[piece * frames : (piece + 1) * frames]
-                    halo_out[piece, q, :, cols] = part_rows.astype(jnp.bfloat16)
+                    halo_out[half, piece, q, :, half_cols] = part_rows.astype(jnp.bfloat16)
                 own[q, :, cols] = total[LEFT:]
 
-    def halo_copy(away):
+    def halo_copy(half, away):
         return remote(
-            halo_out.at[2 - away], halo_in.at[2 - away], h_send.at[away - 1], h_recv.at[away - 1], at(place - away)
+            halo_out.at[half, 2 - away],
+            halo_in.at[half, 2 - away],
+            h_send.at[half, away - 1],
+            h_recv.at[half, away - 1],
+            at(place - away),
         )
 
     def own_to_core(d):
@@ -320,25 +327,27 @@
 
     pairs = width // (2 * HEAD)
     forward_own(0)
+    each(weights, "wait")
     forward_own(1)
-    kv_forward()
     for c in range(CHUNKS):
         forward_x(c)
-        if c == 0:
-            kv_finish()
-            attend(0, pairs // 2)
-            each(weights, "wait")
-        if c == 1:
-            attend(pairs // 2, pairs)
-        if c >= 1:
-            stage_b(c - 1)
-        if c >= 2:
-            stage_c(c - 2)
         gather(c)
         compute(c)
         stage_a(c)
         if c + 2 < CHUNKS:
             forward_own(c + 2)
+        if c >= 1:
+            stage_b(c - 1)
+        if c >= 2:
+            stage_c(c - 2)
+        if c == 1:
+            kv_forward()
+    kv_finish()
+    attend(0, pairs // 2)
+    stage_b(CHUNKS - 1)
+    stage_c(CHUNKS - 2)
+    attend(pairs // 2, pairs)
+    stage_c(CHUNKS - 1)
 
     total_rows = n * 4 * cap
     writes = [
@@ -369,13 +378,8 @@
 
     down_tiles = hidden // TILE
     gate_tiles = width // TILE
-    down_grads(0, down_tiles // 2)
-    stage_b(CHUNKS - 1)
-    stage_c(CHUNKS - 2)
-    down_grads(down_tiles // 2, down_tiles)
+    down_grads(0, down_tiles)
     writes[0].start()
-    stage_c(CHUNKS - 1)
-    gate_grads(0, gate_tiles // 2)
 
     for d in range(1, n):
         home_copy(d).wait_recv()
@@ -387,32 +391,38 @@
     dstream = inverse_rms * (weighted - scaled * jnp.mean(weighted * scaled, -1, keepdims=True))
     sgrad_ref[...] = (grad_ref[...].astype(jnp.float32) + dstream).astype(jnp.bfloat16)
 
-    attend_back()
-    for away in (1, 2):
-        @pl.when(place >= away)
-        def _():
-            halo_copy(away).start()
-
-    gate_grads(gate_tiles // 2, gate_tiles)
+    for half in range(2):
+        attend_back(half)
+        for away in (1, 2):
+            @pl.when(place >= away)
+            def _():
+                halo_copy(half, away).start()
+
+    gate_grads(0, gate_tiles)
     writes[1].start()
 
-    for away in (1, 2):
-        @pl.when(place + away < places)
-        def _():
-            halo_copy(away).wait_recv()
-
-        @pl.when(place + away >= places)
-        def _():
-            halo_in[2 - away] = jnp.zeros_like(halo_in[2 - away])
-
-    for q, out_ref in ((0, gk_ref), (1, gv_ref)):
-        total = own[q] + halo_in[0, q].astype(jnp.float32) + halo_in[1, q].astype(jnp.float32)
-        out_ref[...] = total.astype(jnp.bfloat16)
-
-    for away in (1, 2):
-        @pl.when(place >= away)
-        def _():
-            halo_copy(away).wait_send()
+    wide = width // 2
+    for half in range(2):
+        for away in (1, 2):
+            @pl.when(place + away < places)
+            def _():
+                halo_copy(half, away).wait_recv()
+
+            @pl.when(place + away >= places)
+            def _():
+                halo_in[half, 2 - away] = jnp.zeros_like(halo_in[half, 2 - away])
+
+        for q, out_ref in ((0, gk_ref), (1, gv_ref)):
+            cols = slice(half * wide, (half + 1) * wide)
+            total = own[q, :, cols] + halo_in[half, 0, q].astype(jnp.float32)
+            total = total + halo_in[half, 1, q].astype(jnp.float32)
+            out_ref[:, cols] = total.astype(jnp.bfloat16)
+
+    for half in range(2):
+        for away in (1, 2):
+            @pl.when(place >= away)
+            def _():
+                halo_copy(half, away).wait_send()
 
     @pl.when(has_next)
     def _():
@@ -463,7 +473,7 @@
         ]
         + blocks,
         out_specs=[up_block] + blocks,
-        compiler_params=pltpu.CompilerParams(vmem_limit_bytes=48 * 1024 * 1024),
+        compiler_params=pltpu.CompilerParams(vmem_limit_bytes=62 * 1024 * 1024),
     )(x_rows, dup_rows, *passed)
 
 
@@ -494,8 +504,8 @@
             pltpu.VMEM((frames, width), bf),
             pltpu.VMEM((n, 2, cap, width), bf),
             pltpu.VMEM((2, 3, frames, width), bf),
-            pltpu.VMEM((2, 2, frames, width), bf),
-            pltpu.VMEM((2, 2, frames, width), bf),
+            pltpu.VMEM((2, 2, 2, frames, width // 2), bf),
+            pltpu.VMEM((2, 2, 2, frames, width // 2), bf),
             pltpu.VMEM((2, frames, width), f32),
             pltpu.VMEM((width // (2 * HEAD), 2 * frames, LEFT + frames), f32),
             pltpu.VMEM((n, 4, 2, cap, width), bf),
@@ -523,8 +533,8 @@
             dma((n,)),
             dma((2, 3)),
             dma((2, 2)),
-            dma((2,)),
-            dma((2,)),
+            dma((2, 2)),
+            dma((2, 2)),
         ],
         compiler_params=pltpu.CompilerParams(
             collective_id=0, has_side_effects=True, vmem_limit_bytes=62 * 1024 * 1024

time: 157 us -> 136 us (0.87)
  the two profiles are of different devices: /device:TPU:0 before, /device:TPU:24 now
where the time goes in v3:
time: 136 us; the launch traced here: 135 us
  Pallas kernels  133 us (98%)
  other arithmetic  1.94 us (1%)
    pallas_call x1, Pallas kernels, expert_part(): pl.pallas_call(functools.partial(expert_kernel, n, cap), out_shape=(jax.S...  120 us
    pallas_call x1, Pallas kernels, finish(): pl.pallas_call(finish_kernel, grid=(steps,), out_shape=[jax.ShapeDtypeStr...  12.5 us

profile of v3, /device:TPU:24, one launch (start us, length us, event | category | flops | bytes accessed | tf_op | source)
XLA Modules:
  0.0 135.2 jit_solution(6480701141323660429)
XLA Ops:
  0.6 0.7 convert_bitcast_fusion
  1.3 1.3 pad_maximum_fusion.route_ref
  2.6 120.1 %shard_map.162 = (bf16[128,1024]{1,0:T(8,128)(2,1)}, bf16[128,1024]{1,0:T(8,128)(2,1)}, bf16[128,1024]{1,0:T(8,128)(2,1)}, bf16[128,1024]{1,0:T(8,128)(2,1)}, f3...) custom-call(f32[4,128]{1,0:T(4,128)} %pad_maximum_fusion.route_ref, ...), custom_call_target="tpu_custom_call" | custom-call | flops 25769803776 | bytes 20971520 | tf_op jit(solution)/shard_map/pallas_call | solution.py:488
  122.7 12.5 %shard_map.163 = (f32[1024,1024]{1,0:T(8,128)}, bf16[128,1024]{1,0:T(8,128)(2,1)}, bf16[128,1024]{1,0:T(8,128)(2,1)}, bf16[128,1024]{1,0:T(8,128)(2,1)}, bf16[12...) custom-call(bf16[1536,1024]{1,0:T(8,128)(2,1)} %bitcast.11, ...), custom_call_target="tpu_custom_call" | custom-call | tf_op jit(solution)/shard_map/pallas_call | solution.py:465
